TPU v7x, 256 devices: a whole 4x4x8 slice. The times are simulated.
256 devices in a mesh: freq: 16 (over y_lo, x, core), blk: 16 (over y_hi, z).
Axes of the slice: x: 4, y: 4 (y_hi: 2, y_lo: 2; y = y_hi * 2 + y_lo), z: 8, core: 2. Of those that a mesh axis runs over, the one named last changes fastest.
Arguments:
- samples: bfloat16 [16, 128, 69376], P('blk', 'freq'), may hold values from -6 to 6
- chan_list: int32 [128], replicated, may hold values from 0 to 128, as said below
Outputs:
- visibilities: bfloat16 [128, 16, 9, 2, 128, 128], P('freq', 'blk')
Inputs may be any that keep to these rules, and one draw needn't show every extreme that they name: `chan_list`: 128 distinct bins in increasing order, the first 0 and the last 128.
All inputs are finite; a program needn't handle non-finite values.
Results may differ from a plain program's by a relative error of at most 0.0065.
Values may be sent and summed in bfloat16 or wider, within the bound.
No kernel may reach another device: no remote copies, remote signals or barrier semaphores. Data moves between devices by JAX's collectives and lax.ppermute only.
A program may use at most 64 MiB of HBM per device.

v0:
```python
import jax
import jax.numpy as jnp
from jax import lax
from jax.sharding import PartitionSpec as P

POINTS = 256
TAPS = 16
CHANNELS = 128
SPECTRA = 256


def along_ring(value, steps, other=0):
    half = lax.axis_size("blk") // 2
    pairs = []
    for b in range(2 * half):
        column, plane = (b // half, b % half)
        pairs.append((b, (column + other) % 2 * half + (plane + steps) % half))
    return lax.ppermute(value, "blk", pairs)


def to_twin(value):
    return along_ring(value, 0, 1)


def filter_table(chan_list, freq_size):
    window_len = TAPS * POINTS
    position = jnp.arange(window_len, dtype=jnp.float32)
    offset_pos = (position - window_len / 2 + 0.5) / POINTS
    taper = 0.5 - 0.5 * jnp.cos(2.0 * jnp.pi * (position + 0.5) / window_len)
    window = jnp.sin(jnp.pi * offset_pos) / (jnp.pi * offset_pos) * taper
    window = window / jnp.sqrt(jnp.sum(window * window))
    window = window.reshape(TAPS, 1, POINTS)
    columns = jnp.arange(POINTS, dtype=jnp.int32)
    angles = (chan_list[:, None] * columns[None, :] % POINTS).astype(jnp.float32) * (
        2.0 * jnp.pi / POINTS
    )
    waves = jnp.stack([jnp.cos(angles), -jnp.sin(angles)], axis=0)
    waves = waves.reshape(2, freq_size, 2, -1, POINTS).transpose(2, 1, 0, 3, 4)
    return (window * waves.reshape(1, -1, POINTS)).astype(jnp.bfloat16)


def channelize(frames, filters):
    return lax.conv_general_dilated(
        frames,
        filters,
        window_strides=(1,),
        padding="VALID",
        dimension_numbers=("NWC", "WOI", "CNW"),
        preferred_element_type=jnp.float32,
    ).astype(jnp.bfloat16)


def cross_block(stacked, moving):
    product = lax.dot_general(
        stacked, moving, (((0, 3), (0, 3)), ((1,), (1,))), preferred_element_type=jnp.float32
    )
    chan_count, _, tile = product.shape
    return (product * (1.0 / SPECTRA)).astype(jnp.bfloat16).reshape(chan_count, 2, tile, tile)


def stack_parts(own):
    return jnp.stack(
        [jnp.concatenate([own[0], own[1]], axis=1), jnp.concatenate([own[1], -own[0]], axis=1)]
    )


def body(samples, chan_list):
    freq_size = lax.axis_size("freq")
    half = lax.axis_size("blk") // 2
    column, plane = (lax.axis_index("blk") // half, lax.axis_index("blk") % half)
    inputs = samples.shape[1]
    tile = freq_size * inputs
    frames = samples.reshape(inputs, samples.shape[2] // POINTS, POINTS)
    chans = CHANNELS // freq_size // 2
    voltages = channelize(frames, filter_table(chan_list, freq_size))
    voltages = voltages.reshape(2, freq_size, 2, 1, chans, inputs, SPECTRA)
    kept = lax.dynamic_index_in_dim(voltages, column, 0, keepdims=False)
    given = lax.dynamic_index_in_dim(voltages, 1 - column, 0, keepdims=False)
    pair = jnp.concatenate([kept, to_twin(given)], axis=2)
    pair = lax.all_to_all(pair, "freq", split_axis=0, concat_axis=4, tiled=True)
    lower, upper = (slice(0, chans // 2), slice(chans // 2, chans))
    blocks = {0: pair.reshape(2, 2, chans, tile, SPECTRA)}
    tiles = {}

    def cross(owner, partner, where):
        own, moving = (blocks[owner][:, :, where], blocks[partner][:, :, where])
        swap = (plane + partner) % half > (plane + owner) % half
        return [
            cross_block(
                stack_parts(own[:, block]), jnp.where(swap, moving[:, 1 - block], moving[:, block])
            )
            for block in range(2)
        ]

    def near_tiles(partners):
        made = [cross(0, partner, where) for partner, where in partners]
        moved = to_twin(jnp.stack([both[1] for both in made]))
        for index, (partner, where) in enumerate(partners):
            tiles[-partner % half, where.start] = (made[index][0], moved[index])

    def far_tiles(owner, partner, where):
        both = cross(owner, partner, where)
        tiles[(owner - partner) % half, where.start] = (
            along_ring(both[0], owner),
            along_ring(both[1], owner, 1),
        )

    def step(partner, where=slice(None)):
        way = 1 if partner < 0 else -1
        blocks[partner] = along_ring(blocks[partner + way][:, :, where], way)

    def settle():
        nonlocal tiles, blocks
        tiles, blocks = lax.optimization_barrier((tiles, blocks))

    every = slice(0, chans)
    (step(-1), step(1))
    own = blocks[0]
    made = [
        cross_block(stack_parts(own[:, i]), own[:, i ^ other])
        for other in range(2)
        for i in range(2)
    ]
    moved = to_twin(jnp.stack([made[1], made[3]]))
    tiles[0, 0], tiles[half, 0] = ((made[0], moved[0]), (made[2], moved[1]))
    settle()
    (step(-2), step(2))
    near_tiles([(-1, every), (1, every)])
    settle()
    (step(-3, lower), step(3, upper))
    (far_tiles(-1, 2, lower), far_tiles(1, -2, upper))
    near_tiles([(-2, every), (2, every)])
    settle()
    blocks[-3] = jnp.concatenate([blocks[-3], blocks[-3]], axis=2)
    blocks[3] = jnp.concatenate([blocks[3], blocks[3]], axis=2)
    (far_tiles(1, -3, lower), far_tiles(-1, 3, upper))
    near_tiles([(-3, lower), (3, upper)])

    def whole(place):
        found = []
        for offset in range(half + 1):
            parts = [tiles[key][place] for key in sorted(tiles) if key[0] == offset]
            found.append(parts[0] if len(parts) == 1 else jnp.concatenate(parts, axis=0))
        return jnp.stack(found, axis=1)

    mine, theirs = (whole(0), whole(1))
    low = jnp.where(column == 0, mine, theirs)
    high = jnp.where(column == 0, theirs, mine)
    return jnp.concatenate([low, high], axis=0)[:, None]


def solution(mesh):
    in_specs = (P("blk", "freq", None), P())
    out_specs = P("freq", "blk", None, None, None, None)
    return jax.shard_map(body, mesh=mesh, in_specs=in_specs, out_specs=out_specs, check_vma=False)
```

profile of v0, /device:TPU:6, one launch (start us, length us, event | category | flops | bytes accessed | tf_op | source)
XLA Modules:
  0.0 158.0 jit_solution(9174128341011356209)
XLA Ops:
  0.0 0.7 fusion.207
  0.7 0.8 mul.182
  1.5 1.2 fusion.197
  3.8 4.6 %fusion.3 = bf16[256,8,256]{0,1,2:T(8,128)(2,1)S(1)} fusion(bf16[8,271,256]{2,0,1:T(8,128)(2,1)S(1)} %bitcast.510, f32[256,256]{1,0:T(8,128)S(1)} %mul.188, f32[16,256]{1,0:T(8,128)S(1)} %fusion.199), kind=kOutput, calls=%fused_computation.7 | convolution fusion | flops 4297588736 | bytes 2437120 | tf_op jit(solution)/shard_map/conv_general_dilated | solution.py:43
  8.4 1.3 copy.100
  9.8 3.3 %collective-permute-start = (bf16[16,2,1,4,8,256]{5,4,3,1,0,2:T(8,128)(2,1)S(1)}, bf16[16,2,1,4,8,256]{5,4,3,1,0,2:T(8,128)(2,1)S(1)}, u32[]{:S(2)}, u32[]{:S(2)}) collective-permute-start(bf16[16,2,1,4,8,256]{5,4,3,1,0,2:T(8,128)(2,1)S(1)} %get-tuple-element.144), channel_id=1, source_target_pairs={{0,8},{1,9},{2,10},{3,11},{4,12},{5,13},{6,14},{7,15},{8,0},{9,1},... | collective-permute-start | bytes 1572872 | tf_op jit(solution)/shard_map/ppermute | solution.py:18
  13.0 12.0 %collective-permute-done = bf16[16,2,1,4,8,256]{5,4,3,1,0,2:T(8,128)(2,1)S(1)} collective-permute-done((bf16[16,2,1,4,8,256]{5,4,3,1,0,2:T(8,128)(2,1)S(1)}, bf16[16,2,1,4,8,256]{5,4,3,1,0,2:T(8,128)(2,1)S(1)}, u32[]{:S(2)}, u32[]{:S(2)}) %collective-permute-start) | collective-permute-done | bytes 524320 | tf_op jit(solution)/shard_map/ppermute | solution.py:18
  25.2 19.2 %all_to_all.15 = bf16[16,2,2,4,8,256]{5,4,3,1,2,0:T(8,128)(2,1)S(1)} all-to-all(bf16[16,2,2,4,8,256]{5,4,3,1,2,0:T(8,128)(2,1)S(1)} %copy.101), channel_id=1, replica_groups=mesh['freq'=16,'blk'=16] {'freq'}, dimensions={0} | all-to-all | bytes 2097152 | tf_op jit(solution)/shard_map/all_to_all | solution.py:80
  44.7 2.0 %collective-permute-start.2 = (bf16[2,2,4,128,256]{4,3,2,0,1:T(8,128)(2,1)S(1)}, bf16[2,2,4,128,256]{4,3,2,0,1:T(8,128)(2,1)S(1)}, u32[]{:S(2)}, u32[]{:S(2)}) collective-permute-start(bf16[2,2,4,128,256]{4,3,2,0,1:T(8,128)(2,1)S(1)} %copy_bitcast_fusion), channel_id=1, source_target_pairs={{0,1},{1,2},{2,3},{3,4},{4,5},{5,6},{6,7},{7,0},{8,9},{9,10},{10,1... | collective-permute-start | bytes 3145736 | tf_op jit(solution)/shard_map/ppermute | solution.py:18
  46.7 4.0 %collective-permute-start.3 = (bf16[2,2,4,128,256]{4,3,2,0,1:T(8,128)(2,1)S(1)}, bf16[2,2,4,128,256]{4,3,2,0,1:T(8,128)(2,1)}, u32[]{:S(2)}, u32[]{:S(2)}) collective-permute-start(bf16[2,2,4,128,256]{4,3,2,0,1:T(8,128)(2,1)S(1)} %copy_bitcast_fusion), channel_id=1, source_target_pairs={{0,7},{1,0},{2,1},{3,2},{4,3},{5,4},{6,5},{7,6},{8,15},{9,8},{10,9... | collective-permute-start | bytes 3145736 | tf_op jit(solution)/shard_map/ppermute | solution.py:18
  50.7 1.1 maximum_bitcast_fusion.1
  51.8 0.4 fusion.26
  52.3 0.4 fusion.25
  52.7 0.8 pad_maximum_fusion.19
  53.6 2.9 %collective-permute-start.1 = (bf16[2,4,2,128,128]{4,3,2,1,0:T(8,128)(2,1)}, bf16[2,4,2,128,128]{4,3,2,1,0:T(8,128)(2,1)}, u32[]{:S(2)}, u32[]{:S(2)}) collective-permute-start(bf16[2,4,2,128,128]{4,3,2,1,0:T(8,128)(2,1)} %pad_maximum_fusion.19), channel_id=1, source_target_pairs={{0,8},{1,9},{2,10},{3,11},{4,12},{5,13},{6,14},{7,15},{8,0},{9,1},... | collective-permute-start | bytes 1572872 | tf_op jit(solution)/shard_map/ppermute | solution.py:18
  56.5 1.7 %fusion.24 = bf16[4,256,128]{2,1,0:T(8,128)(2,1)S(1)} fusion(bf16[1,4,256,256]{3,2,1,0:T(8,128)(2,1)} %get-tuple-element.164, bf16[1,4,256,256]{3,2,1,0:T(8,128)(2,1)} %get-tuple-element.163, bf16[2,2,4,128,256]{4,3,2,0,1:T(8,128)(2,1)S(1)} %copy_bitcast_fusion), kind=kOutput, calls=%fused_computation.40 | convolution fusion | flops 135004160 | bytes 1835008 | tf_op jit(solution)/shard_map/dot_general | solution.py:54
  58.2 0.4 fusion.27
  58.7 10.9 %collective-permute-done.1 = bf16[2,4,2,128,128]{4,3,2,1,0:T(8,128)(2,1)} collective-permute-done((bf16[2,4,2,128,128]{4,3,2,1,0:T(8,128)(2,1)}, bf16[2,4,2,128,128]{4,3,2,1,0:T(8,128)(2,1)}, u32[]{:S(2)}, u32[]{:S(2)}) %collective-permute-start.1) | collective-permute-done | bytes 524320 | tf_op jit(solution)/shard_map/ppermute | solution.py:18
  69.6 1.1 slice_bitcast_fusion.14
  70.7 3.9 %collective-permute-done.2 = bf16[2,2,4,128,256]{4,3,2,0,1:T(8,128)(2,1)S(1)} collective-permute-done((bf16[2,2,4,128,256]{4,3,2,0,1:T(8,128)(2,1)S(1)}, bf16[2,2,4,128,256]{4,3,2,0,1:T(8,128)(2,1)S(1)}, u32[]{:S(2)}, u32[]{:S(2)}) %collective-permute-start.2) | collective-permute-done | bytes 1048608 | tf_op jit(solution)/shard_map/ppermute | solution.py:18
  75.0 3.2 %collective-permute-start.6 = (bf16[2,2,4,128,256]{4,3,2,0,1:T(8,128)(2,1)}, bf16[2,2,4,128,256]{4,3,2,0,1:T(8,128)(2,1)S(1)}, u32[]{:S(2)}, u32[]{:S(2)}) collective-permute-start(bf16[2,2,4,128,256]{4,3,2,0,1:T(8,128)(2,1)} %collective-permute-done.3), channel_id=1, source_target_pairs={{0,7},{1,0},{2,1},{3,2},{4,3},{5,4},{6,5},{7,6},{8,15},{9,8},{10,9... | collective-permute-start | bytes 3145736 | tf_op jit(solution)/shard_map/ppermute | solution.py:18
  78.3 0.4 fusion.22
  78.8 1.7 %fusion.21 = bf16[4,256,128]{2,1,0:T(8,128)(2,1)S(1)} fusion(bf16[1,4,256,256]{3,2,1,0:T(8,128)(2,1)S(1)} %get-tuple-element.158, bf16[1,4,256,256]{3,2,1,0:T(8,128)(2,1)S(1)} %get-tuple-element.157, pred[]{:T(512)S(6)} %gt.31, bf16[2,2,4,128,256]{4,3,2,0,1:T(8,128)(2,1)} %collective-permute-done.3), kind=kOutput, calls=%fused_computation.37 | convolution fusion | flops 135266304 | bytes 2359297 | tf_op jit(solution)/shard_map/dot_general | solution.py:54
  80.5 3.0 %collective-permute-start.4 = (bf16[2,4,2,128,128]{4,3,2,1,0:T(8,128)(2,1)S(1)}, bf16[2,4,2,128,128]{4,3,2,1,0:T(8,128)(2,1)S(1)}, u32[]{:S(2)}, u32[]{:S(2)}) collective-permute-start(bf16[2,4,2,128,128]{4,3,2,1,0:T(8,128)(2,1)S(1)} %pad_maximum_fusion.20), channel_id=1, source_target_pairs={{0,8},{1,9},{2,10},{3,11},{4,12},{5,13},{6,14},{7,15},{8,0},{9,1},... | collective-permute-start | bytes 1572872 | tf_op jit(solution)/shard_map/ppermute | solution.py:18
  83.6 1.7 %fusion.20 = bf16[4,256,128]{2,1,0:T(8,128)(2,1)S(1)} fusion(bf16[1,4,256,256]{3,2,1,0:T(8,128)(2,1)S(1)} %get-tuple-element.160, bf16[1,4,256,256]{3,2,1,0:T(8,128)(2,1)S(1)} %get-tuple-element.159, pred[]{:T(512)S(6)} %gt.31, bf16[2,2,4,128,256]{4,3,2,0,1:T(8,128)(2,1)} %collective-permute-done.3), kind=kOutput, calls=%fused_computation.36 | convolution fusion | flops 135266304 | bytes 2359297 | tf_op jit(solution)/shard_map/dot_general | solution.py:54
  85.3 0.4 fusion.23
  85.8 9.7 %collective-permute-done.4 = bf16[2,4,2,128,128]{4,3,2,1,0:T(8,128)(2,1)S(1)} collective-permute-done((bf16[2,4,2,128,128]{4,3,2,1,0:T(8,128)(2,1)S(1)}, bf16[2,4,2,128,128]{4,3,2,1,0:T(8,128)(2,1)S(1)}, u32[]{:S(2)}, u32[]{:S(2)}) %collective-permute-start.4) | collective-permute-done | bytes 524320 | tf_op jit(solution)/shard_map/ppermute | solution.py:18
  95.5 5.8 %collective-permute-done.5 = bf16[2,2,4,128,256]{4,3,2,0,1:T(8,128)(2,1)S(1)} collective-permute-done((bf16[2,2,4,128,256]{4,3,2,0,1:T(8,128)(2,1)S(1)}, bf16[2,2,4,128,256]{4,3,2,0,1:T(8,128)(2,1)S(1)}, u32[]{:S(2)}, u32[]{:S(2)}) %collective-permute-start.5) | collective-permute-done | bytes 1048608 | tf_op jit(solution)/shard_map/ppermute | solution.py:18
  101.7 1.0 slice_bitcast_fusion.36
  102.7 1.0 slice_bitcast_fusion.48
  103.6 1.0 fusion.233
  104.9 0.5 fusion.16
  105.3 0.5 fusion.17
  105.8 0.5 fusion.18
  106.2 0.5 fusion.19
  106.8 0.3 fusion.43
  107.2 5.6 %collective-permute-start.11 = (bf16[2,2,128,128]{3,2,1,0:T(8,128)(2,1)S(1)}, bf16[2,2,128,128]{3,2,1,0:T(8,128)(2,1)S(1)}, u32[]{:S(2)}, u32[]{:S(2)}) collective-permute-start(bf16[2,2,128,128]{3,2,1,0:T(8,128)(2,1)S(1)} %bitcast.532), channel_id=1, source_target_pairs={{0,15},{1,8},{2,9},{3,10},{4,11},{5,12},{6,13},{7,14},{8,7},{9,0},... | collective-permute-start | bytes 393224 | tf_op jit(solution)/shard_map/ppermute | solution.py:18
  112.8 0.3 fusion.42
  113.1 0.5 collective-permute-start.10
  113.7 0.7 collective-permute-start.7
  114.4 1.6 %collective-permute-start.12 = (bf16[2,2,2,128,256]{4,3,2,0,1:T(8,128)(2,1)S(1)}, bf16[2,2,2,128,256]{4,3,2,0,1:T(8,128)(2,1)S(1)}, u32[]{:S(2)}, u32[]{:S(2)}) collective-permute-start(bf16[2,2,2,128,256]{4,3,2,0,1:T(8,128)(2,1)S(1)} %slice.438), channel_id=1, source_target_pairs={{0,1},{1,2},{2,3},{3,4},{4,5},{5,6},{6,7},{7,0},{8,9},{9,10},{10,1... | collective-permute-start | bytes 1572872 | tf_op jit(solution)/shard_map/ppermute | solution.py:18
  116.0 1.7 %collective-permute-start.13 = (bf16[2,2,2,128,256]{4,3,2,0,1:T(8,128)(2,1)S(1)}, bf16[2,2,2,128,256]{4,3,2,0,1:T(8,128)(2,1)S(1)}, u32[]{:S(2)}, u32[]{:S(2)}) collective-permute-start(bf16[2,2,2,128,256]{4,3,2,0,1:T(8,128)(2,1)S(1)} %slice.439), channel_id=1, source_target_pairs={{0,7},{1,0},{2,1},{3,2},{4,3},{5,4},{6,5},{7,6},{8,15},{9,8},{10,9... | collective-permute-start | bytes 1572872 | tf_op jit(solution)/shard_map/ppermute | solution.py:18
  118.0 0.3 fusion.40
  118.3 2.8 %collective-permute-start.9 = (bf16[2,2,128,128]{3,2,1,0:T(8,128)(2,1)S(1)}, bf16[2,2,128,128]{3,2,1,0:T(8,128)(2,1)S(1)}, u32[]{:S(2)}, u32[]{:S(2)}) collective-permute-start(bf16[2,2,128,128]{3,2,1,0:T(8,128)(2,1)S(1)} %bitcast.534), channel_id=1, source_target_pairs={{0,9},{1,10},{2,11},{3,12},{4,13},{5,14},{6,15},{7,8},{8,1},{9,2},... | collective-permute-start | bytes 393224 | tf_op jit(solution)/shard_map/ppermute | solution.py:18
  121.1 6.9 %collective-permute-done.7 = bf16[2,4,2,128,128]{4,3,2,1,0:T(8,128)(2,1)S(1)} collective-permute-done((bf16[2,4,2,128,128]{4,3,2,1,0:T(8,128)(2,1)S(1)}, bf16[2,4,2,128,128]{4,3,2,1,0:T(8,128)(2,1)S(1)}, u32[]{:S(2)}, u32[]{:S(2)}) %collective-permute-start.7) | collective-permute-done | bytes 524320 | tf_op jit(solution)/shard_map/ppermute | solution.py:18
  128.0 2.4 %collective-permute-start.8 = (bf16[2,2,128,128]{3,2,1,0:T(8,128)(2,1)S(1)}, bf16[2,2,128,128]{3,2,1,0:T(8,128)(2,1)S(1)}, u32[]{:S(2)}, u32[]{:S(2)}) collective-permute-start(bf16[2,2,128,128]{3,2,1,0:T(8,128)(2,1)S(1)} %bitcast.535), channel_id=1, source_target_pairs={{0,1},{1,2},{2,3},{3,4},{4,5},{5,6},{6,7},{7,0},{8,9},{9,10},{10,1... | collective-permute-start | bytes 393224 | tf_op jit(solution)/shard_map/ppermute | solution.py:18
  130.5 3.3 %collective-permute-done.9 = bf16[2,2,128,128]{3,2,1,0:T(8,128)(2,1)S(1)} collective-permute-done((bf16[2,2,128,128]{3,2,1,0:T(8,128)(2,1)S(1)}, bf16[2,2,128,128]{3,2,1,0:T(8,128)(2,1)S(1)}, u32[]{:S(2)}, u32[]{:S(2)}) %collective-permute-start.9) | collective-permute-done | bytes 131104 | tf_op jit(solution)/shard_map/ppermute | solution.py:18
  133.8 1.5 collective-permute-done.8
  135.3 1.0 slice_bitcast_fusion.32
  136.3 1.0 slice_bitcast_fusion.44
  137.3 1.0 fusion.237
  138.7 0.3 fusion.50
  139.0 2.6 %collective-permute-start.17 = (bf16[2,2,128,128]{3,2,1,0:T(8,128)(2,1)S(1)}, bf16[2,2,128,128]{3,2,1,0:T(8,128)(2,1)S(1)}, u32[]{:S(2)}, u32[]{:S(2)}) collective-permute-start(bf16[2,2,128,128]{3,2,1,0:T(8,128)(2,1)S(1)} %bitcast.528), channel_id=1, source_target_pairs={{0,9},{1,10},{2,11},{3,12},{4,13},{5,14},{6,15},{7,8},{8,1},{9,2},... | collective-permute-start | bytes 393224 | tf_op jit(solution)/shard_map/ppermute | solution.py:18
  141.6 0.3 fusion.51
  141.9 3.4 %collective-permute-start.18 = (bf16[2,2,128,128]{3,2,1,0:T(8,128)(2,1)S(1)}, bf16[2,2,128,128]{3,2,1,0:T(8,128)(2,1)S(1)}, u32[]{:S(2)}, u32[]{:S(2)}) collective-permute-start(bf16[2,2,128,128]{3,2,1,0:T(8,128)(2,1)S(1)} %bitcast.529), channel_id=1, source_target_pairs={{0,15},{1,8},{2,9},{3,10},{4,11},{5,12},{6,13},{7,14},{8,7},{9,0},... | collective-permute-start | bytes 393224 | tf_op jit(solution)/shard_map/ppermute | solution.py:18
  145.4 0.3 fusion.48
  145.8 0.3 fusion.49
  146.1 1.5 collective-permute-start.16
  148.0 0.3 collective-permute-start.14
  148.3 0.3 fusion.46
  148.7 3.1 %collective-permute-start.15 = (bf16[2,2,128,128]{3,2,1,0:T(8,128)(2,1)S(1)}, bf16[2,2,128,128]{3,2,1,0:T(8,128)(2,1)S(1)}, u32[]{:S(2)}, u32[]{:S(2)}) collective-permute-start(bf16[2,2,128,128]{3,2,1,0:T(8,128)(2,1)S(1)} %bitcast.533), channel_id=1, source_target_pairs={{0,7},{1,0},{2,1},{3,2},{4,3},{5,4},{6,5},{7,6},{8,15},{9,8},{10,9... | collective-permute-start | bytes 393224 | tf_op jit(solution)/shard_map/ppermute | solution.py:18
  152.3 0.3 fusion.44
  152.7 1.5 collective-permute-done.14
  155.4 2.6 %maximum_bitcast_fusion = bf16[8,1,9,2,128,128]{5,4,3,2,1,0:T(8,128)(2,1)} fusion(bf16[4,9,2,128,128]{4,3,2,1,0:T(8,128)(2,1)S(1)} %get-tuple-element.88, bf16[4,9,2,128,128]{4,3,2,1,0:T(8,128)(2,1)S(1)} %get-tuple-element.87), kind=kLoop, calls=%fused_computation | loop fusion | flops 2359296 | bytes 9437184 | tf_op jit(solution)/shard_map/broadcast_in_dim | solution.py:149
  (88 shorter events, 5.0 us)
Async XLA Ops:
  0.0 3.7 %copy-start = (bf16[1,8,69376]{2,1,0:T(8,128)(2,1)S(1)}, bf16[1,8,69376]{2,1,0:T(8,128)(2,1)}, u32[]{:S(2)}) copy-start(bf16[1,8,69376]{2,1,0:T(8,128)(2,1)} %param.2) | copy-start | bytes 3330052
  9.8 15.3 %collective-permute-start = (bf16[16,2,1,4,8,256]{5,4,3,1,0,2:T(8,128)(2,1)S(1)}, bf16[16,2,1,4,8,256]{5,4,3,1,0,2:T(8,128)(2,1)S(1)}, u32[]{:S(2)}, u32[]{:S(2)}) collective-permute-start(bf16[16,2,1,4,8,256]{5,4,3,1,0,2:T(8,128)(2,1)S(1)} %get-tuple-element.144), channel_id=1, source_target_pairs={{0,8},{1,9},{2,10},{3,11},{4,12},{5,13},{6,14},{7,15},{8,0},{9,1},... | collective-permute-start | bytes 1572872 | tf_op jit(solution)/shard_map/ppermute | solution.py:18
  44.7 29.9 %collective-permute-start.2 = (bf16[2,2,4,128,256]{4,3,2,0,1:T(8,128)(2,1)S(1)}, bf16[2,2,4,128,256]{4,3,2,0,1:T(8,128)(2,1)S(1)}, u32[]{:S(2)}, u32[]{:S(2)}) collective-permute-start(bf16[2,2,4,128,256]{4,3,2,0,1:T(8,128)(2,1)S(1)} %copy_bitcast_fusion), channel_id=1, source_target_pairs={{0,1},{1,2},{2,3},{3,4},{4,5},{5,6},{6,7},{7,0},{8,9},{9,10},{10,1... | collective-permute-start | bytes 3145736 | tf_op jit(solution)/shard_map/ppermute | solution.py:18
  46.7 27.9 %collective-permute-start.3 = (bf16[2,2,4,128,256]{4,3,2,0,1:T(8,128)(2,1)S(1)}, bf16[2,2,4,128,256]{4,3,2,0,1:T(8,128)(2,1)}, u32[]{:S(2)}, u32[]{:S(2)}) collective-permute-start(bf16[2,2,4,128,256]{4,3,2,0,1:T(8,128)(2,1)S(1)} %copy_bitcast_fusion), channel_id=1, source_target_pairs={{0,7},{1,0},{2,1},{3,2},{4,3},{5,4},{6,5},{7,6},{8,15},{9,8},{10,9... | collective-permute-start | bytes 3145736 | tf_op jit(solution)/shard_map/ppermute | solution.py:18
  53.6 16.0 %collective-permute-start.1 = (bf16[2,4,2,128,128]{4,3,2,1,0:T(8,128)(2,1)}, bf16[2,4,2,128,128]{4,3,2,1,0:T(8,128)(2,1)}, u32[]{:S(2)}, u32[]{:S(2)}) collective-permute-start(bf16[2,4,2,128,128]{4,3,2,1,0:T(8,128)(2,1)} %pad_maximum_fusion.19), channel_id=1, source_target_pairs={{0,8},{1,9},{2,10},{3,11},{4,12},{5,13},{6,14},{7,15},{8,0},{9,1},... | collective-permute-start | bytes 1572872 | tf_op jit(solution)/shard_map/ppermute | solution.py:18
  56.5 1.7 %copy-start.1 = (bf16[1,4,256,256]{3,2,1,0:T(8,128)(2,1)S(1)}, bf16[1,4,256,256]{3,2,1,0:T(8,128)(2,1)}, u32[]{:S(2)}) copy-start(bf16[1,4,256,256]{3,2,1,0:T(8,128)(2,1)} %get-tuple-element.163) | copy-start | bytes 1572868
  56.5 1.7 %copy-start.2 = (bf16[1,4,256,256]{3,2,1,0:T(8,128)(2,1)S(1)}, bf16[1,4,256,256]{3,2,1,0:T(8,128)(2,1)}, u32[]{:S(2)}) copy-start(bf16[1,4,256,256]{3,2,1,0:T(8,128)(2,1)} %get-tuple-element.164) | copy-start | bytes 1572868
  74.8 26.6 %collective-permute-start.5 = (bf16[2,2,4,128,256]{4,3,2,0,1:T(8,128)(2,1)S(1)}, bf16[2,2,4,128,256]{4,3,2,0,1:T(8,128)(2,1)S(1)}, u32[]{:S(2)}, u32[]{:S(2)}) collective-permute-start(bf16[2,2,4,128,256]{4,3,2,0,1:T(8,128)(2,1)S(1)} %collective-permute-done.2), channel_id=1, source_target_pairs={{0,1},{1,2},{2,3},{3,4},{4,5},{5,6},{6,7},{7,0},{8,9},{9,10},{10,1... | collective-permute-start | bytes 3145736 | tf_op jit(solution)/shard_map/ppermute | solution.py:18
  75.0 26.3 %collective-permute-start.6 = (bf16[2,2,4,128,256]{4,3,2,0,1:T(8,128)(2,1)}, bf16[2,2,4,128,256]{4,3,2,0,1:T(8,128)(2,1)S(1)}, u32[]{:S(2)}, u32[]{:S(2)}) collective-permute-start(bf16[2,2,4,128,256]{4,3,2,0,1:T(8,128)(2,1)} %collective-permute-done.3), channel_id=1, source_target_pairs={{0,7},{1,0},{2,1},{3,2},{4,3},{5,4},{6,5},{7,6},{8,15},{9,8},{10,9... | collective-permute-start | bytes 3145736 | tf_op jit(solution)/shard_map/ppermute | solution.py:18
  80.5 15.0 %collective-permute-start.4 = (bf16[2,4,2,128,128]{4,3,2,1,0:T(8,128)(2,1)S(1)}, bf16[2,4,2,128,128]{4,3,2,1,0:T(8,128)(2,1)S(1)}, u32[]{:S(2)}, u32[]{:S(2)}) collective-permute-start(bf16[2,4,2,128,128]{4,3,2,1,0:T(8,128)(2,1)S(1)} %pad_maximum_fusion.20), channel_id=1, source_target_pairs={{0,8},{1,9},{2,10},{3,11},{4,12},{5,13},{6,14},{7,15},{8,0},{9,1},... | collective-permute-start | bytes 1572872 | tf_op jit(solution)/shard_map/ppermute | solution.py:18
  107.2 11.2 %collective-permute-start.11 = (bf16[2,2,128,128]{3,2,1,0:T(8,128)(2,1)S(1)}, bf16[2,2,128,128]{3,2,1,0:T(8,128)(2,1)S(1)}, u32[]{:S(2)}, u32[]{:S(2)}) collective-permute-start(bf16[2,2,128,128]{3,2,1,0:T(8,128)(2,1)S(1)} %bitcast.532), channel_id=1, source_target_pairs={{0,15},{1,8},{2,9},{3,10},{4,11},{5,12},{6,13},{7,14},{8,7},{9,0},... | collective-permute-start | bytes 393224 | tf_op jit(solution)/shard_map/ppermute | solution.py:18
  113.1 17.4 %collective-permute-start.10 = (bf16[2,2,128,128]{3,2,1,0:T(8,128)(2,1)S(1)}, bf16[2,2,128,128]{3,2,1,0:T(8,128)(2,1)S(1)}, u32[]{:S(2)}, u32[]{:S(2)}) collective-permute-start(bf16[2,2,128,128]{3,2,1,0:T(8,128)(2,1)S(1)} %bitcast.531), channel_id=1, source_target_pairs={{0,7},{1,0},{2,1},{3,2},{4,3},{5,4},{6,5},{7,6},{8,15},{9,8},{10,9... | collective-permute-start | bytes 393224 | tf_op jit(solution)/shard_map/ppermute | solution.py:18
  113.7 14.3 %collective-permute-start.7 = (bf16[2,4,2,128,128]{4,3,2,1,0:T(8,128)(2,1)S(1)}, bf16[2,4,2,128,128]{4,3,2,1,0:T(8,128)(2,1)S(1)}, u32[]{:S(2)}, u32[]{:S(2)}) collective-permute-start(bf16[2,4,2,128,128]{4,3,2,1,0:T(8,128)(2,1)S(1)} %pad_maximum_fusion.21), channel_id=1, source_target_pairs={{0,8},{1,9},{2,10},{3,11},{4,12},{5,13},{6,14},{7,15},{8,0},{9,1},... | collective-permute-start | bytes 1572872 | tf_op jit(solution)/shard_map/ppermute | solution.py:18
  114.4 20.9 %collective-permute-start.12 = (bf16[2,2,2,128,256]{4,3,2,0,1:T(8,128)(2,1)S(1)}, bf16[2,2,2,128,256]{4,3,2,0,1:T(8,128)(2,1)S(1)}, u32[]{:S(2)}, u32[]{:S(2)}) collective-permute-start(bf16[2,2,2,128,256]{4,3,2,0,1:T(8,128)(2,1)S(1)} %slice.438), channel_id=1, source_target_pairs={{0,1},{1,2},{2,3},{3,4},{4,5},{5,6},{6,7},{7,0},{8,9},{9,10},{10,1... | collective-permute-start | bytes 1572872 | tf_op jit(solution)/shard_map/ppermute | solution.py:18
  116.0 19.4 %collective-permute-start.13 = (bf16[2,2,2,128,256]{4,3,2,0,1:T(8,128)(2,1)S(1)}, bf16[2,2,2,128,256]{4,3,2,0,1:T(8,128)(2,1)S(1)}, u32[]{:S(2)}, u32[]{:S(2)}) collective-permute-start(bf16[2,2,2,128,256]{4,3,2,0,1:T(8,128)(2,1)S(1)} %slice.439), channel_id=1, source_target_pairs={{0,7},{1,0},{2,1},{3,2},{4,3},{5,4},{6,5},{7,6},{8,15},{9,8},{10,9... | collective-permute-start | bytes 1572872 | tf_op jit(solution)/shard_map/ppermute | solution.py:18
  118.3 15.5 %collective-permute-start.9 = (bf16[2,2,128,128]{3,2,1,0:T(8,128)(2,1)S(1)}, bf16[2,2,128,128]{3,2,1,0:T(8,128)(2,1)S(1)}, u32[]{:S(2)}, u32[]{:S(2)}) collective-permute-start(bf16[2,2,128,128]{3,2,1,0:T(8,128)(2,1)S(1)} %bitcast.534), channel_id=1, source_target_pairs={{0,9},{1,10},{2,11},{3,12},{4,13},{5,14},{6,15},{7,8},{8,1},{9,2},... | collective-permute-start | bytes 393224 | tf_op jit(solution)/shard_map/ppermute | solution.py:18
  128.0 7.3 %collective-permute-start.8 = (bf16[2,2,128,128]{3,2,1,0:T(8,128)(2,1)S(1)}, bf16[2,2,128,128]{3,2,1,0:T(8,128)(2,1)S(1)}, u32[]{:S(2)}, u32[]{:S(2)}) collective-permute-start(bf16[2,2,128,128]{3,2,1,0:T(8,128)(2,1)S(1)} %bitcast.535), channel_id=1, source_target_pairs={{0,1},{1,2},{2,3},{3,4},{4,5},{5,6},{6,7},{7,0},{8,9},{9,10},{10,1... | collective-permute-start | bytes 393224 | tf_op jit(solution)/shard_map/ppermute | solution.py:18
  139.0 15.8 %collective-permute-start.17 = (bf16[2,2,128,128]{3,2,1,0:T(8,128)(2,1)S(1)}, bf16[2,2,128,128]{3,2,1,0:T(8,128)(2,1)S(1)}, u32[]{:S(2)}, u32[]{:S(2)}) collective-permute-start(bf16[2,2,128,128]{3,2,1,0:T(8,128)(2,1)S(1)} %bitcast.528), channel_id=1, source_target_pairs={{0,9},{1,10},{2,11},{3,12},{4,13},{5,14},{6,15},{7,8},{8,1},{9,2},... | collective-permute-start | bytes 393224 | tf_op jit(solution)/shard_map/ppermute | solution.py:18
  141.9 12.9 %collective-permute-start.18 = (bf16[2,2,128,128]{3,2,1,0:T(8,128)(2,1)S(1)}, bf16[2,2,128,128]{3,2,1,0:T(8,128)(2,1)S(1)}, u32[]{:S(2)}, u32[]{:S(2)}) collective-permute-start(bf16[2,2,128,128]{3,2,1,0:T(8,128)(2,1)S(1)} %bitcast.529), channel_id=1, source_target_pairs={{0,15},{1,8},{2,9},{3,10},{4,11},{5,12},{6,13},{7,14},{8,7},{9,0},... | collective-permute-start | bytes 393224 | tf_op jit(solution)/shard_map/ppermute | solution.py:18
  146.1 8.6 %collective-permute-start.16 = (bf16[2,2,2,128,128]{4,3,2,1,0:T(8,128)(2,1)S(1)}, bf16[2,2,2,128,128]{4,3,2,1,0:T(8,128)(2,1)S(1)}, u32[]{:S(2)}, u32[]{:S(2)}) collective-permute-start(bf16[2,2,2,128,128]{4,3,2,1,0:T(8,128)(2,1)S(1)} %pad_maximum_fusion.22), channel_id=1, source_target_pairs={{0,8},{1,9},{2,10},{3,11},{4,12},{5,13},{6,14},{7,15},{8,0},{9,1},... | collective-permute-start | bytes 786440 | tf_op jit(solution)/shard_map/ppermute | solution.py:18
  148.0 6.3 %collective-permute-start.14 = (bf16[2,2,128,128]{3,2,1,0:T(8,128)(2,1)S(1)}, bf16[2,2,128,128]{3,2,1,0:T(8,128)(2,1)S(1)}, u32[]{:S(2)}, u32[]{:S(2)}) collective-permute-start(bf16[2,2,128,128]{3,2,1,0:T(8,128)(2,1)S(1)} %bitcast.530), channel_id=1, source_target_pairs={{0,1},{1,2},{2,3},{3,4},{4,5},{5,6},{6,7},{7,0},{8,9},{9,10},{10,1... | collective-permute-start | bytes 393224 | tf_op jit(solution)/shard_map/ppermute | solution.py:18
  148.7 5.6 %collective-permute-start.15 = (bf16[2,2,128,128]{3,2,1,0:T(8,128)(2,1)S(1)}, bf16[2,2,128,128]{3,2,1,0:T(8,128)(2,1)S(1)}, u32[]{:S(2)}, u32[]{:S(2)}) collective-permute-start(bf16[2,2,128,128]{3,2,1,0:T(8,128)(2,1)S(1)} %bitcast.533), channel_id=1, source_target_pairs={{0,7},{1,0},{2,1},{3,2},{4,3},{5,4},{6,5},{7,6},{8,15},{9,8},{10,9... | collective-permute-start | bytes 393224 | tf_op jit(solution)/shard_map/ppermute | solution.py:18
where the time goes:
time: 158 us
  waiting for transfers between devices  55.9 us (35%)
  starting transfers between devices  44.8 us (28%)
  blocking collectives  19.2 us (12%)
  matrix products  17.4 us (11%)
  other arithmetic  10.7 us (7%)
  local copies, waits for them, and re-layouts  8.39 us (5%)
    ppermute x19, waiting for transfers between devices, along_ring(): return lax.ppermute(value, 'blk', pairs)  55.9 us
    ppermute x19, starting transfers between devices, along_ring(): return lax.ppermute(value, 'blk', pairs)  44.8 us
    all_to_all x1, blocking collectives, body(): pair = lax.all_to_all(pair, 'freq', split_axis=0, concat_axis=4, tiled=True)  19.2 us
    dot_general x24, matrix products, cross_block(): lax.dot_general(stacked, moving, (((0, 3), (0, 3)), ((1,), (1,))), prefer...  12.8 us
    conv_general_dilated x1, matrix products, channelize(): lax.conv_general_dilated(frames, filters, window_strides=(1,), padding='V...  4.6 us
  transfers between devices with their start and end apart: 19, of which 10 were waited for; matrix products, arithmetic and copies ran while one was open for 9% of the time, Pallas kernels for 0%

commit v1 on v0

--- a/solution.py
+++ b/solution.py
@@ -77,7 +77,10 @@
     kept = lax.dynamic_index_in_dim(voltages, column, 0, keepdims=False)
     given = lax.dynamic_index_in_dim(voltages, 1 - column, 0, keepdims=False)
     pair = jnp.concatenate([kept, to_twin(given)], axis=2)
-    pair = lax.all_to_all(pair, "freq", split_axis=0, concat_axis=4, tiled=True)
+    pair = jnp.concatenate(
+        lax.all_to_all(jnp.stack(jnp.split(pair, lax.axis_size("freq"), axis=0)), "freq", 0, 0),
+        axis=4,
+    )
     lower, upper = (slice(0, chans // 2), slice(chans // 2, chans))
     blocks = {0: pair.reshape(2, 2, chans, tile, SPECTRA)}
     tiles = {}

time: 158 us -> 152 us (0.962)
  waiting for transfers between devices: 55.9 us -> 60.1 us
  local copies, waits for them, and re-layouts: 8.39 us -> 4.52 us
  starting transfers between devices: 44.8 us -> 41.3 us
  matrix products: 17.4 us -> 14.9 us
    ppermute x19, waiting for transfers between devices: 55.9 us -> 60.1 us  [along_ring(): return lax.ppermute(value, 'blk', pairs)]
    ppermute x19, starting transfers between devices: 44.8 us -> 41.3 us  [along_ring(): return lax.ppermute(value, 'blk', pairs)]
    dot_general x24, matrix products: 12.8 us -> 10.3 us  [cross_block(): lax.dot_general(stacked, moving, (((0, 3), (0, 3)), ((1,), (1,))), prefer...]
    neg x8, other arithmetic: 2.46 us -> 0.51 us  [stack_parts(): -own[0]]
    squeeze x7, local copies, waits for them, and re-layouts: 2.12 us -> 0.19 us  [stack_parts(): own[1]]
    squeeze x8, local copies, waits for them, and re-layouts: 2.19 us -> 0.27 us  [stack_parts(): own[0]]
  transfers between devices with their start and end apart: 19 -> 19, of which waited for: 10 -> 8; matrix products, arithmetic and copies ran while one was open for 9% -> 10% of each run, Pallas kernels for 0% -> 0%
where the time goes in v1:
time: 152 us; the launch traced here: 151 us
  waiting for transfers between devices  60.1 us (40%)
  starting transfers between devices  41.3 us (27%)
  blocking collectives  19.2 us (13%)
  matrix products  14.9 us (10%)
  other arithmetic  9.34 us (6%)
  local copies, waits for them, and re-layouts  4.52 us (3%)
  between operations  1.78 us (1%)
    ppermute x19, waiting for transfers between devices, along_ring(): return lax.ppermute(value, 'blk', pairs)  60.1 us
    ppermute x19, starting transfers between devices, along_ring(): return lax.ppermute(value, 'blk', pairs)  41.3 us
    all_to_all x1, blocking collectives, body(): lax.all_to_all(jnp.stack(jnp.split(pair, lax.axis_size('freq'), axis=0)),...  19.2 us
    dot_general x24, matrix products, cross_block(): lax.dot_general(stacked, moving, (((0, 3), (0, 3)), ((1,), (1,))), prefer...  10.3 us
    conv_general_dilated x1, matrix products, channelize(): lax.conv_general_dilated(frames, filters, window_strides=(1,), padding='V...  4.6 us
  transfers between devices with their start and end apart: 19, of which 8 were waited for; matrix products, arithmetic and copies ran while one was open for 10% of the time, Pallas kernels for 0%

profile of v1, /device:TPU:6, one launch (start us, length us, event | category | flops | bytes accessed | tf_op | source)
XLA Modules:
  0.0 151.2 jit_solution(17163117490520248902)
XLA Ops:
  0.0 0.7 fusion.147
  0.7 0.8 mul.182
  1.5 1.2 fusion.137
  2.8 0.1 mul.188
  3.6 0.1 fusion.139
  3.8 4.6 %fusion.3 = bf16[256,8,256]{0,1,2:T(8,128)(2,1)S(1)} fusion(bf16[8,271,256]{2,0,1:T(8,128)(2,1)S(1)} %bitcast.548, f32[256,256]{1,0:T(8,128)S(1)} %mul.188, f32[16,256]{1,0:T(8,128)S(1)} %fusion.139), kind=kOutput, calls=%fused_computation.37 | convolution fusion | flops 4297588736 | bytes 2437120 | tf_op jit(solution)/shard_map/conv_general_dilated | solution.py:43
  8.4 1.3 copy.66
  9.7 3.3 %collective-permute-start = (bf16[16,2,1,4,8,256]{5,4,3,1,0,2:T(8,128)(2,1)S(1)}, bf16[16,2,1,4,8,256]{5,4,3,1,0,2:T(8,128)(2,1)S(1)}, u32[]{:S(2)}, u32[]{:S(2)}) collective-permute-start(bf16[16,2,1,4,8,256]{5,4,3,1,0,2:T(8,128)(2,1)S(1)} %get-tuple-element.158), channel_id=1, source_target_pairs={{0,8},{1,9},{2,10},{3,11},{4,12},{5,13},{6,14},{7,15},{8,0},{9,1},... | collective-permute-start | bytes 1572872 | tf_op jit(solution)/shard_map/ppermute | solution.py:18
  13.0 12.0 %collective-permute-done = bf16[16,2,1,4,8,256]{5,4,3,1,0,2:T(8,128)(2,1)S(1)} collective-permute-done((bf16[16,2,1,4,8,256]{5,4,3,1,0,2:T(8,128)(2,1)S(1)}, bf16[16,2,1,4,8,256]{5,4,3,1,0,2:T(8,128)(2,1)S(1)}, u32[]{:S(2)}, u32[]{:S(2)}) %collective-permute-start) | collective-permute-done | bytes 524320 | tf_op jit(solution)/shard_map/ppermute | solution.py:18
  25.2 19.2 %all_to_all.5 = bf16[16,1,2,2,4,8,256]{6,5,4,2,3,1,0:T(8,128)(2,1)S(1)} all-to-all(bf16[16,1,2,2,4,8,256]{6,5,4,2,3,1,0:T(8,128)(2,1)S(1)} %constant_dynamic-update-slice_fusion), channel_id=1, replica_groups=mesh['freq'=16,'blk'=16] {'freq'}, dimensions={0} | all-to-all | bytes 2097152 | tf_op jit(solution)/shard_map/all_to_all | solution.py:81
  44.4 0.1 copy_bitcast_fusion
  44.8 2.0 %collective-permute-start.2 = (bf16[2,2,4,128,256]{4,3,0,2,1:T(8,128)(2,1)S(1)}, bf16[2,2,4,128,256]{4,3,0,2,1:T(8,128)(2,1)S(1)}, u32[]{:S(2)}, u32[]{:S(2)}) collective-permute-start(bf16[2,2,4,128,256]{4,3,0,2,1:T(8,128)(2,1)S(1)} %copy_bitcast_fusion), channel_id=1, source_target_pairs={{0,1},{1,2},{2,3},{3,4},{4,5},{5,6},{6,7},{7,0},{8,9},{9,10},{10,1... | collective-permute-start | bytes 3145736 | tf_op jit(solution)/shard_map/ppermute | solution.py:18
  46.8 4.0 %collective-permute-start.3 = (bf16[2,2,4,128,256]{4,3,0,2,1:T(8,128)(2,1)S(1)}, bf16[2,2,4,128,256]{4,3,0,2,1:T(8,128)(2,1)S(1)}, u32[]{:S(2)}, u32[]{:S(2)}) collective-permute-start(bf16[2,2,4,128,256]{4,3,0,2,1:T(8,128)(2,1)S(1)} %copy_bitcast_fusion), channel_id=1, source_target_pairs={{0,7},{1,0},{2,1},{3,2},{4,3},{5,4},{6,5},{7,6},{8,15},{9,8},{10,9... | collective-permute-start | bytes 3145736 | tf_op jit(solution)/shard_map/ppermute | solution.py:18
  50.8 1.1 maximum_bitcast_fusion.1
  52.0 0.4 fusion.26
  52.4 0.4 fusion.25
  52.9 0.9 pad_maximum_fusion.18
  53.7 2.9 %collective-permute-start.1 = (bf16[2,4,2,128,128]{4,3,2,1,0:T(8,128)(2,1)}, bf16[2,4,2,128,128]{4,3,2,1,0:T(8,128)(2,1)}, u32[]{:S(2)}, u32[]{:S(2)}) collective-permute-start(bf16[2,4,2,128,128]{4,3,2,1,0:T(8,128)(2,1)} %pad_maximum_fusion.18), channel_id=1, source_target_pairs={{0,8},{1,9},{2,10},{3,11},{4,12},{5,13},{6,14},{7,15},{8,0},{9,1},... | collective-permute-start | bytes 1572872 | tf_op jit(solution)/shard_map/ppermute | solution.py:18
  56.7 1.9 %fusion.24 = bf16[4,256,128]{2,1,0:T(8,128)(2,1)S(1)} fusion(bf16[1,4,256,256]{3,2,1,0:T(8,128)(2,1)} %get-tuple-element.186, bf16[1,4,256,256]{3,2,1,0:T(8,128)(2,1)} %get-tuple-element.185, bf16[2,4,128,256]{3,2,0,1:T(8,128)(2,1)} %copy-done.6), kind=kOutput, calls=%fused_computation.70 | convolution fusion | flops 135004160 | bytes 1835008 | tf_op jit(solution)/shard_map/dot_general | solution.py:54
  58.6 0.4 fusion.27
  59.0 10.7 %collective-permute-done.1 = bf16[2,4,2,128,128]{4,3,2,1,0:T(8,128)(2,1)} collective-permute-done((bf16[2,4,2,128,128]{4,3,2,1,0:T(8,128)(2,1)}, bf16[2,4,2,128,128]{4,3,2,1,0:T(8,128)(2,1)}, u32[]{:S(2)}, u32[]{:S(2)}) %collective-permute-start.1) | collective-permute-done | bytes 524320 | tf_op jit(solution)/shard_map/ppermute | solution.py:18
  69.7 1.1 slice_bitcast_fusion.10
  70.8 3.9 %collective-permute-done.2 = bf16[2,2,4,128,256]{4,3,0,2,1:T(8,128)(2,1)S(1)} collective-permute-done((bf16[2,2,4,128,256]{4,3,0,2,1:T(8,128)(2,1)S(1)}, bf16[2,2,4,128,256]{4,3,0,2,1:T(8,128)(2,1)S(1)}, u32[]{:S(2)}, u32[]{:S(2)}) %collective-permute-start.2) | collective-permute-done | bytes 1048608 | tf_op jit(solution)/shard_map/ppermute | solution.py:18
  74.8 0.1 fusion.187
  74.9 3.3 %collective-permute-start.6 = (bf16[2,2,4,128,256]{4,3,0,2,1:T(8,128)(2,1)S(1)}, bf16[2,2,4,128,256]{4,3,0,2,1:T(8,128)(2,1)S(1)}, u32[]{:S(2)}, u32[]{:S(2)}) collective-permute-start(bf16[2,2,4,128,256]{4,3,0,2,1:T(8,128)(2,1)S(1)} %collective-permute-done.3), channel_id=1, source_target_pairs={{0,7},{1,0},{2,1},{3,2},{4,3},{5,4},{6,5},{7,6},{8,15},{9,8},{10,9... | collective-permute-start | bytes 3145736 | tf_op jit(solution)/shard_map/ppermute | solution.py:18
  78.5 0.4 fusion.22
  79.0 0.4 fusion.21
  79.5 3.0 %collective-permute-start.4 = (bf16[2,4,2,128,128]{4,3,2,1,0:T(8,128)(2,1)S(1)}, bf16[2,4,2,128,128]{4,3,2,1,0:T(8,128)(2,1)S(1)}, u32[]{:S(2)}, u32[]{:S(2)}) collective-permute-start(bf16[2,4,2,128,128]{4,3,2,1,0:T(8,128)(2,1)S(1)} %pad_maximum_fusion.19), channel_id=1, source_target_pairs={{0,8},{1,9},{2,10},{3,11},{4,12},{5,13},{6,14},{7,15},{8,0},{9,1},... | collective-permute-start | bytes 1572872 | tf_op jit(solution)/shard_map/ppermute | solution.py:18
  82.6 0.4 fusion.20
  83.0 0.4 fusion.23
  83.4 11.0 %collective-permute-done.4 = bf16[2,4,2,128,128]{4,3,2,1,0:T(8,128)(2,1)S(1)} collective-permute-done((bf16[2,4,2,128,128]{4,3,2,1,0:T(8,128)(2,1)S(1)}, bf16[2,4,2,128,128]{4,3,2,1,0:T(8,128)(2,1)S(1)}, u32[]{:S(2)}, u32[]{:S(2)}) %collective-permute-start.4) | collective-permute-done | bytes 524320 | tf_op jit(solution)/shard_map/ppermute | solution.py:18
  94.5 9.7 %collective-permute-done.5 = bf16[2,2,4,128,256]{4,3,0,2,1:T(8,128)(2,1)S(1)} collective-permute-done((bf16[2,2,4,128,256]{4,3,0,2,1:T(8,128)(2,1)S(1)}, bf16[2,2,4,128,256]{4,3,0,2,1:T(8,128)(2,1)S(1)}, u32[]{:S(2)}, u32[]{:S(2)}) %collective-permute-start.5) | collective-permute-done | bytes 1048608 | tf_op jit(solution)/shard_map/ppermute | solution.py:18
  104.8 0.3 fusion.43
  105.1 2.5 %collective-permute-start.11 = (bf16[2,2,128,128]{3,2,1,0:T(8,128)(2,1)S(1)}, bf16[2,2,128,128]{3,2,1,0:T(8,128)(2,1)S(1)}, u32[]{:S(2)}, u32[]{:S(2)}) collective-permute-start(bf16[2,2,128,128]{3,2,1,0:T(8,128)(2,1)S(1)} %bitcast.569), channel_id=1, source_target_pairs={{0,15},{1,8},{2,9},{3,10},{4,11},{5,12},{6,13},{7,14},{8,7},{9,0},... | collective-permute-start | bytes 393224 | tf_op jit(solution)/shard_map/ppermute | solution.py:18
  107.6 0.3 fusion.42
  108.3 0.4 fusion.18
  108.7 0.4 fusion.17
  109.2 0.7 collective-permute-start.7
  110.1 0.4 fusion.16
  110.5 0.4 fusion.19
  110.9 2.1 %collective-permute-start.12 = (bf16[2,2,2,128,256]{4,3,0,2,1:T(8,128)(2,1)S(1)}, bf16[2,2,2,128,256]{4,3,0,2,1:T(8,128)(2,1)S(1)}, u32[]{:S(2)}, u32[]{:S(2)}) collective-permute-start(bf16[2,2,2,128,256]{4,3,0,2,1:T(8,128)(2,1)S(1)} %slice.438), channel_id=1, source_target_pairs={{0,1},{1,2},{2,3},{3,4},{4,5},{5,6},{6,7},{7,0},{8,9},{9,10},{10,1... | collective-permute-start | bytes 1572872 | tf_op jit(solution)/shard_map/ppermute | solution.py:18
  113.0 1.2 collective-permute-start.13
  114.3 0.3 fusion.41
  114.6 0.3 fusion.40
  115.0 3.2 %collective-permute-start.9 = (bf16[2,2,128,128]{3,2,1,0:T(8,128)(2,1)S(1)}, bf16[2,2,128,128]{3,2,1,0:T(8,128)(2,1)S(1)}, u32[]{:S(2)}, u32[]{:S(2)}) collective-permute-start(bf16[2,2,128,128]{3,2,1,0:T(8,128)(2,1)S(1)} %bitcast.572), channel_id=1, source_target_pairs={{0,9},{1,10},{2,11},{3,12},{4,13},{5,14},{6,15},{7,8},{8,1},{9,2},... | collective-permute-start | bytes 393224 | tf_op jit(solution)/shard_map/ppermute | solution.py:18
  118.2 6.1 %collective-permute-done.7 = bf16[2,4,2,128,128]{4,3,2,1,0:T(8,128)(2,1)S(1)} collective-permute-done((bf16[2,4,2,128,128]{4,3,2,1,0:T(8,128)(2,1)S(1)}, bf16[2,4,2,128,128]{4,3,2,1,0:T(8,128)(2,1)S(1)}, u32[]{:S(2)}, u32[]{:S(2)}) %collective-permute-start.7) | collective-permute-done | bytes 524320 | tf_op jit(solution)/shard_map/ppermute | solution.py:18
  124.3 1.5 collective-permute-start.8
  125.8 5.2 %collective-permute-done.9 = bf16[2,2,128,128]{3,2,1,0:T(8,128)(2,1)S(1)} collective-permute-done((bf16[2,2,128,128]{3,2,1,0:T(8,128)(2,1)S(1)}, bf16[2,2,128,128]{3,2,1,0:T(8,128)(2,1)S(1)}, u32[]{:S(2)}, u32[]{:S(2)}) %collective-permute-start.9) | collective-permute-done | bytes 131104 | tf_op jit(solution)/shard_map/ppermute | solution.py:18
  131.3 0.1 fusion.179
  131.5 0.3 fusion.50
  131.8 2.2 %collective-permute-start.17 = (bf16[2,2,128,128]{3,2,1,0:T(8,128)(2,1)S(1)}, bf16[2,2,128,128]{3,2,1,0:T(8,128)(2,1)S(1)}, u32[]{:S(2)}, u32[]{:S(2)}) collective-permute-start(bf16[2,2,128,128]{3,2,1,0:T(8,128)(2,1)S(1)} %bitcast.566), channel_id=1, source_target_pairs={{0,9},{1,10},{2,11},{3,12},{4,13},{5,14},{6,15},{7,8},{8,1},{9,2},... | collective-permute-start | bytes 393224 | tf_op jit(solution)/shard_map/ppermute | solution.py:18
  134.2 0.3 fusion.51
  134.5 3.8 %collective-permute-start.18 = (bf16[2,2,128,128]{3,2,1,0:T(8,128)(2,1)S(1)}, bf16[2,2,128,128]{3,2,1,0:T(8,128)(2,1)S(1)}, u32[]{:S(2)}, u32[]{:S(2)}) collective-permute-start(bf16[2,2,128,128]{3,2,1,0:T(8,128)(2,1)S(1)} %bitcast.567), channel_id=1, source_target_pairs={{0,15},{1,8},{2,9},{3,10},{4,11},{5,12},{6,13},{7,14},{8,7},{9,0},... | collective-permute-start | bytes 393224 | tf_op jit(solution)/shard_map/ppermute | solution.py:18
  138.3 0.3 fusion.48
  138.7 0.3 fusion.49
  139.0 2.0 %collective-permute-start.16 = (bf16[2,2,2,128,128]{4,3,2,1,0:T(8,128)(2,1)S(1)}, bf16[2,2,2,128,128]{4,3,2,1,0:T(8,128)(2,1)S(1)}, u32[]{:S(2)}, u32[]{:S(2)}) collective-permute-start(bf16[2,2,2,128,128]{4,3,2,1,0:T(8,128)(2,1)S(1)} %pad_maximum_fusion.21), channel_id=1, source_target_pairs={{0,8},{1,9},{2,10},{3,11},{4,12},{5,13},{6,14},{7,15},{8,0},{9,1},... | collective-permute-start | bytes 786440 | tf_op jit(solution)/shard_map/ppermute | solution.py:18
  141.1 0.3 fusion.45
  141.6 0.3 fusion.46
  141.9 3.3 %collective-permute-start.15 = (bf16[2,2,128,128]{3,2,1,0:T(8,128)(2,1)S(1)}, bf16[2,2,128,128]{3,2,1,0:T(8,128)(2,1)S(1)}, u32[]{:S(2)}, u32[]{:S(2)}) collective-permute-start(bf16[2,2,128,128]{3,2,1,0:T(8,128)(2,1)S(1)} %bitcast.571), channel_id=1, source_target_pairs={{0,7},{1,0},{2,1},{3,2},{4,3},{5,4},{6,5},{7,6},{8,15},{9,8},{10,9... | collective-permute-start | bytes 393224 | tf_op jit(solution)/shard_map/ppermute | solution.py:18
  145.4 0.3 fusion.47
  145.8 0.3 fusion.44
  146.1 1.6 %collective-permute-done.14 = bf16[2,2,128,128]{3,2,1,0:T(8,128)(2,1)S(1)} collective-permute-done((bf16[2,2,128,128]{3,2,1,0:T(8,128)(2,1)S(1)}, bf16[2,2,128,128]{3,2,1,0:T(8,128)(2,1)S(1)}, u32[]{:S(2)}, u32[]{:S(2)}) %collective-permute-start.14) | collective-permute-done | bytes 131104 | tf_op jit(solution)/shard_map/ppermute | solution.py:18
  148.2 0.3 broadcast_select_fusion.1
  148.6 2.6 %maximum_bitcast_fusion = bf16[8,1,9,2,128,128]{5,4,3,2,1,0:T(8,128)(2,1)} fusion(bf16[4,9,2,128,128]{4,3,2,1,0:T(8,128)(2,1)S(1)} %get-tuple-element.88, bf16[4,9,2,128,128]{4,3,2,1,0:T(8,128)(2,1)S(1)} %get-tuple-element.87), kind=kLoop, calls=%fused_computation | loop fusion | flops 2359296 | bytes 9437184 | tf_op jit(solution)/shard_map/broadcast_in_dim | solution.py:152
  (119 shorter events, 3.7 us)
Async XLA Ops:
  0.0 3.7 %copy-start = (bf16[1,8,69376]{2,1,0:T(8,128)(2,1)S(1)}, bf16[1,8,69376]{2,1,0:T(8,128)(2,1)}, u32[]{:S(2)}) copy-start(bf16[1,8,69376]{2,1,0:T(8,128)(2,1)} %param.2) | copy-start | bytes 3330052
  9.7 15.3 %collective-permute-start = (bf16[16,2,1,4,8,256]{5,4,3,1,0,2:T(8,128)(2,1)S(1)}, bf16[16,2,1,4,8,256]{5,4,3,1,0,2:T(8,128)(2,1)S(1)}, u32[]{:S(2)}, u32[]{:S(2)}) collective-permute-start(bf16[16,2,1,4,8,256]{5,4,3,1,0,2:T(8,128)(2,1)S(1)} %get-tuple-element.158), channel_id=1, source_target_pairs={{0,8},{1,9},{2,10},{3,11},{4,12},{5,13},{6,14},{7,15},{8,0},{9,1},... | collective-permute-start | bytes 1572872 | tf_op jit(solution)/shard_map/ppermute | solution.py:18
  44.8 7.6 %copy-start.6 = (bf16[2,4,128,256]{3,2,0,1:T(8,128)(2,1)}, bf16[2,4,128,256]{3,2,0,1:T(8,128)(2,1)S(1)}, u32[]{:S(2)}) copy-start(bf16[2,4,128,256]{3,2,0,1:T(8,128)(2,1)S(1)} %get-tuple-element.149) | copy-start | bytes 1572868
  44.8 7.6 %copy-start.4 = (bf16[2,4,128,256]{3,2,0,1:T(8,128)(2,1)}, bf16[2,4,128,256]{3,2,0,1:T(8,128)(2,1)S(1)}, u32[]{:S(2)}) copy-start(bf16[2,4,128,256]{3,2,0,1:T(8,128)(2,1)S(1)} %get-tuple-element.150) | copy-start | bytes 1572868
  44.8 29.9 %collective-permute-start.2 = (bf16[2,2,4,128,256]{4,3,0,2,1:T(8,128)(2,1)S(1)}, bf16[2,2,4,128,256]{4,3,0,2,1:T(8,128)(2,1)S(1)}, u32[]{:S(2)}, u32[]{:S(2)}) collective-permute-start(bf16[2,2,4,128,256]{4,3,0,2,1:T(8,128)(2,1)S(1)} %copy_bitcast_fusion), channel_id=1, source_target_pairs={{0,1},{1,2},{2,3},{3,4},{4,5},{5,6},{6,7},{7,0},{8,9},{9,10},{10,1... | collective-permute-start | bytes 3145736 | tf_op jit(solution)/shard_map/ppermute | solution.py:18
  46.8 27.9 %collective-permute-start.3 = (bf16[2,2,4,128,256]{4,3,0,2,1:T(8,128)(2,1)S(1)}, bf16[2,2,4,128,256]{4,3,0,2,1:T(8,128)(2,1)S(1)}, u32[]{:S(2)}, u32[]{:S(2)}) collective-permute-start(bf16[2,2,4,128,256]{4,3,0,2,1:T(8,128)(2,1)S(1)} %copy_bitcast_fusion), channel_id=1, source_target_pairs={{0,7},{1,0},{2,1},{3,2},{4,3},{5,4},{6,5},{7,6},{8,15},{9,8},{10,9... | collective-permute-start | bytes 3145736 | tf_op jit(solution)/shard_map/ppermute | solution.py:18
  53.7 16.0 %collective-permute-start.1 = (bf16[2,4,2,128,128]{4,3,2,1,0:T(8,128)(2,1)}, bf16[2,4,2,128,128]{4,3,2,1,0:T(8,128)(2,1)}, u32[]{:S(2)}, u32[]{:S(2)}) collective-permute-start(bf16[2,4,2,128,128]{4,3,2,1,0:T(8,128)(2,1)} %pad_maximum_fusion.18), channel_id=1, source_target_pairs={{0,8},{1,9},{2,10},{3,11},{4,12},{5,13},{6,14},{7,15},{8,0},{9,1},... | collective-permute-start | bytes 1572872 | tf_op jit(solution)/shard_map/ppermute | solution.py:18
  56.6 1.9 %copy-start.2 = (bf16[1,4,256,256]{3,2,1,0:T(8,128)(2,1)S(1)}, bf16[1,4,256,256]{3,2,1,0:T(8,128)(2,1)}, u32[]{:S(2)}) copy-start(bf16[1,4,256,256]{3,2,1,0:T(8,128)(2,1)} %get-tuple-element.185) | copy-start | bytes 1572868
  56.7 1.9 %copy-start.3 = (bf16[1,4,256,256]{3,2,1,0:T(8,128)(2,1)S(1)}, bf16[1,4,256,256]{3,2,1,0:T(8,128)(2,1)}, u32[]{:S(2)}) copy-start(bf16[1,4,256,256]{3,2,1,0:T(8,128)(2,1)} %get-tuple-element.186) | copy-start | bytes 1572868
  56.7 1.9 %copy-start.5 = (bf16[2,4,128,256]{3,2,0,1:T(8,128)(2,1)S(1)}, bf16[2,4,128,256]{3,2,0,1:T(8,128)(2,1)}, u32[]{:S(2)}) copy-start(bf16[2,4,128,256]{3,2,0,1:T(8,128)(2,1)} %copy-done.4) | copy-start | bytes 1572868
  74.9 29.2 %collective-permute-start.6 = (bf16[2,2,4,128,256]{4,3,0,2,1:T(8,128)(2,1)S(1)}, bf16[2,2,4,128,256]{4,3,0,2,1:T(8,128)(2,1)S(1)}, u32[]{:S(2)}, u32[]{:S(2)}) collective-permute-start(bf16[2,2,4,128,256]{4,3,0,2,1:T(8,128)(2,1)S(1)} %collective-permute-done.3), channel_id=1, source_target_pairs={{0,7},{1,0},{2,1},{3,2},{4,3},{5,4},{6,5},{7,6},{8,15},{9,8},{10,9... | collective-permute-start | bytes 3145736 | tf_op jit(solution)/shard_map/ppermute | solution.py:18
  78.3 25.9 %collective-permute-start.5 = (bf16[2,2,4,128,256]{4,3,0,2,1:T(8,128)(2,1)S(1)}, bf16[2,2,4,128,256]{4,3,0,2,1:T(8,128)(2,1)S(1)}, u32[]{:S(2)}, u32[]{:S(2)}) collective-permute-start(bf16[2,2,4,128,256]{4,3,0,2,1:T(8,128)(2,1)S(1)} %collective-permute-done.2), channel_id=1, source_target_pairs={{0,1},{1,2},{2,3},{3,4},{4,5},{5,6},{6,7},{7,0},{8,9},{9,10},{10,1... | collective-permute-start | bytes 3145736 | tf_op jit(solution)/shard_map/ppermute | solution.py:18
  79.5 14.9 %collective-permute-start.4 = (bf16[2,4,2,128,128]{4,3,2,1,0:T(8,128)(2,1)S(1)}, bf16[2,4,2,128,128]{4,3,2,1,0:T(8,128)(2,1)S(1)}, u32[]{:S(2)}, u32[]{:S(2)}) collective-permute-start(bf16[2,4,2,128,128]{4,3,2,1,0:T(8,128)(2,1)S(1)} %pad_maximum_fusion.19), channel_id=1, source_target_pairs={{0,8},{1,9},{2,10},{3,11},{4,12},{5,13},{6,14},{7,15},{8,0},{9,1},... | collective-permute-start | bytes 1572872 | tf_op jit(solution)/shard_map/ppermute | solution.py:18
  105.1 9.9 %collective-permute-start.11 = (bf16[2,2,128,128]{3,2,1,0:T(8,128)(2,1)S(1)}, bf16[2,2,128,128]{3,2,1,0:T(8,128)(2,1)S(1)}, u32[]{:S(2)}, u32[]{:S(2)}) collective-permute-start(bf16[2,2,128,128]{3,2,1,0:T(8,128)(2,1)S(1)} %bitcast.569), channel_id=1, source_target_pairs={{0,15},{1,8},{2,9},{3,10},{4,11},{5,12},{6,13},{7,14},{8,7},{9,0},... | collective-permute-start | bytes 393224 | tf_op jit(solution)/shard_map/ppermute | solution.py:18
  107.9 17.8 %collective-permute-start.10 = (bf16[2,2,128,128]{3,2,1,0:T(8,128)(2,1)S(1)}, bf16[2,2,128,128]{3,2,1,0:T(8,128)(2,1)S(1)}, u32[]{:S(2)}, u32[]{:S(2)}) collective-permute-start(bf16[2,2,128,128]{3,2,1,0:T(8,128)(2,1)S(1)} %bitcast.568), channel_id=1, source_target_pairs={{0,7},{1,0},{2,1},{3,2},{4,3},{5,4},{6,5},{7,6},{8,15},{9,8},{10,9... | collective-permute-start | bytes 393224 | tf_op jit(solution)/shard_map/ppermute | solution.py:18
  109.2 15.0 %collective-permute-start.7 = (bf16[2,4,2,128,128]{4,3,2,1,0:T(8,128)(2,1)S(1)}, bf16[2,4,2,128,128]{4,3,2,1,0:T(8,128)(2,1)S(1)}, u32[]{:S(2)}, u32[]{:S(2)}) collective-permute-start(bf16[2,4,2,128,128]{4,3,2,1,0:T(8,128)(2,1)S(1)} %pad_maximum_fusion.20), channel_id=1, source_target_pairs={{0,8},{1,9},{2,10},{3,11},{4,12},{5,13},{6,14},{7,15},{8,0},{9,1},... | collective-permute-start | bytes 1572872 | tf_op jit(solution)/shard_map/ppermute | solution.py:18
  110.9 20.0 %collective-permute-start.12 = (bf16[2,2,2,128,256]{4,3,0,2,1:T(8,128)(2,1)S(1)}, bf16[2,2,2,128,256]{4,3,0,2,1:T(8,128)(2,1)S(1)}, u32[]{:S(2)}, u32[]{:S(2)}) collective-permute-start(bf16[2,2,2,128,256]{4,3,0,2,1:T(8,128)(2,1)S(1)} %slice.438), channel_id=1, source_target_pairs={{0,1},{1,2},{2,3},{3,4},{4,5},{5,6},{6,7},{7,0},{8,9},{9,10},{10,1... | collective-permute-start | bytes 1572872 | tf_op jit(solution)/shard_map/ppermute | solution.py:18
  113.0 18.0 %collective-permute-start.13 = (bf16[2,2,2,128,256]{4,3,0,2,1:T(8,128)(2,1)S(1)}, bf16[2,2,2,128,256]{4,3,0,2,1:T(8,128)(2,1)S(1)}, u32[]{:S(2)}, u32[]{:S(2)}) collective-permute-start(bf16[2,2,2,128,256]{4,3,0,2,1:T(8,128)(2,1)S(1)} %slice.439), channel_id=1, source_target_pairs={{0,7},{1,0},{2,1},{3,2},{4,3},{5,4},{6,5},{7,6},{8,15},{9,8},{10,9... | collective-permute-start | bytes 1572872 | tf_op jit(solution)/shard_map/ppermute | solution.py:18
  115.0 16.0 %collective-permute-start.9 = (bf16[2,2,128,128]{3,2,1,0:T(8,128)(2,1)S(1)}, bf16[2,2,128,128]{3,2,1,0:T(8,128)(2,1)S(1)}, u32[]{:S(2)}, u32[]{:S(2)}) collective-permute-start(bf16[2,2,128,128]{3,2,1,0:T(8,128)(2,1)S(1)} %bitcast.572), channel_id=1, source_target_pairs={{0,9},{1,10},{2,11},{3,12},{4,13},{5,14},{6,15},{7,8},{8,1},{9,2},... | collective-permute-start | bytes 393224 | tf_op jit(solution)/shard_map/ppermute | solution.py:18
  124.3 6.7 %collective-permute-start.8 = (bf16[2,2,128,128]{3,2,1,0:T(8,128)(2,1)S(1)}, bf16[2,2,128,128]{3,2,1,0:T(8,128)(2,1)S(1)}, u32[]{:S(2)}, u32[]{:S(2)}) collective-permute-start(bf16[2,2,128,128]{3,2,1,0:T(8,128)(2,1)S(1)} %bitcast.573), channel_id=1, source_target_pairs={{0,1},{1,2},{2,3},{3,4},{4,5},{5,6},{6,7},{7,0},{8,9},{9,10},{10,1... | collective-permute-start | bytes 393224 | tf_op jit(solution)/shard_map/ppermute | solution.py:18
  131.8 16.2 %collective-permute-start.17 = (bf16[2,2,128,128]{3,2,1,0:T(8,128)(2,1)S(1)}, bf16[2,2,128,128]{3,2,1,0:T(8,128)(2,1)S(1)}, u32[]{:S(2)}, u32[]{:S(2)}) collective-permute-start(bf16[2,2,128,128]{3,2,1,0:T(8,128)(2,1)S(1)} %bitcast.566), channel_id=1, source_target_pairs={{0,9},{1,10},{2,11},{3,12},{4,13},{5,14},{6,15},{7,8},{8,1},{9,2},... | collective-permute-start | bytes 393224 | tf_op jit(solution)/shard_map/ppermute | solution.py:18
  134.5 13.5 %collective-permute-start.18 = (bf16[2,2,128,128]{3,2,1,0:T(8,128)(2,1)S(1)}, bf16[2,2,128,128]{3,2,1,0:T(8,128)(2,1)S(1)}, u32[]{:S(2)}, u32[]{:S(2)}) collective-permute-start(bf16[2,2,128,128]{3,2,1,0:T(8,128)(2,1)S(1)} %bitcast.567), channel_id=1, source_target_pairs={{0,15},{1,8},{2,9},{3,10},{4,11},{5,12},{6,13},{7,14},{8,7},{9,0},... | collective-permute-start | bytes 393224 | tf_op jit(solution)/shard_map/ppermute | solution.py:18
  139.0 8.9 %collective-permute-start.16 = (bf16[2,2,2,128,128]{4,3,2,1,0:T(8,128)(2,1)S(1)}, bf16[2,2,2,128,128]{4,3,2,1,0:T(8,128)(2,1)S(1)}, u32[]{:S(2)}, u32[]{:S(2)}) collective-permute-start(bf16[2,2,2,128,128]{4,3,2,1,0:T(8,128)(2,1)S(1)} %pad_maximum_fusion.21), channel_id=1, source_target_pairs={{0,8},{1,9},{2,10},{3,11},{4,12},{5,13},{6,14},{7,15},{8,0},{9,1},... | collective-permute-start | bytes 786440 | tf_op jit(solution)/shard_map/ppermute | solution.py:18
  141.4 6.3 %collective-permute-start.14 = (bf16[2,2,128,128]{3,2,1,0:T(8,128)(2,1)S(1)}, bf16[2,2,128,128]{3,2,1,0:T(8,128)(2,1)S(1)}, u32[]{:S(2)}, u32[]{:S(2)}) collective-permute-start(bf16[2,2,128,128]{3,2,1,0:T(8,128)(2,1)S(1)} %bitcast.570), channel_id=1, source_target_pairs={{0,1},{1,2},{2,3},{3,4},{4,5},{5,6},{6,7},{7,0},{8,9},{9,10},{10,1... | collective-permute-start | bytes 393224 | tf_op jit(solution)/shard_map/ppermute | solution.py:18
  141.9 5.8 %collective-permute-start.15 = (bf16[2,2,128,128]{3,2,1,0:T(8,128)(2,1)S(1)}, bf16[2,2,128,128]{3,2,1,0:T(8,128)(2,1)S(1)}, u32[]{:S(2)}, u32[]{:S(2)}) collective-permute-start(bf16[2,2,128,128]{3,2,1,0:T(8,128)(2,1)S(1)} %bitcast.571), channel_id=1, source_target_pairs={{0,7},{1,0},{2,1},{3,2},{4,3},{5,4},{6,5},{7,6},{8,15},{9,8},{10,9... | collective-permute-start | bytes 393224 | tf_op jit(solution)/shard_map/ppermute | solution.py:18
  148.5 2.6 %copy-start.1 = (bf16[1,8,69376]{2,1,0:T(8,128)(2,1)S(1)}, bf16[1,8,69376]{2,1,0:T(8,128)(2,1)}, u32[]{:S(2)}) copy-start(bf16[1,8,69376]{2,1,0:T(8,128)(2,1)} %param.2) | copy-start | bytes 3330052
